TPU v7x, 1024 devices: a whole 4x4x32 slice. The times are simulated.
1024 devices in a mesh: graph: 64 (over z, core), replica: 16 (over x, y).
Axes of the slice: x: 4, y: 4, z: 32, core: 2. Of those that a mesh axis runs over, the one named last changes fastest.
Arguments:
- features: bfloat16 [16, 8192, 512], P('replica', 'graph'), may hold values from -8 to 8
- neighbours: int32 [16, 8192, 16], P('replica', 'graph'), may hold values from 0 to 255
- send_rows: int32 [16, 64, 64, 2], P('replica', 'graph'), may hold values from 0 to 127
- send_counts: int32 [16, 64, 64], P('replica', 'graph'), may hold values from 0 to 2, as said below
- candidates: int32 [16, 2048, 512], P('replica', 'graph'), may hold values from 0 to 127
- perturbation: float32 [16, 2048, 4, 512], P('replica', 'graph'), may hold values from -320 to 320
- weight: bfloat16 [512, 512], replicated, may hold values from -0.25 to 0.25
Outputs:
- d_features: bfloat16 [16, 8192, 512], P('replica', 'graph')
- weight_grad: float32 [512, 512], P('graph', 'replica')
Inputs may be any that keep to these rules, and one draw needn't show every extreme that they name: `send_counts`: rows that one device sends to another in its mini-batch; in every draw one device of each mini-batch receives 2 rows from every device.
All inputs are finite; a program needn't handle non-finite values.
Results may differ from a plain program's by a relative error of at most 0.013.
Values may be sent and summed in bfloat16 or wider, within the bound.
A program may use at most 32 MiB of HBM per device.

v0:
```python
import math

import jax
import jax.numpy as jnp
from jax import lax
from jax.sharding import PartitionSpec as P

TOP = 20


SCORE_SCALE = 16.0
LOSS_SCALE = 16.0
EPSILON = 1e-05


def embed_backward(mean_rows, weight, candidates, perturbation):
    query_count = candidates.shape[0]
    pre = jnp.dot(mean_rows, weight, preferred_element_type=jnp.float32)
    inverse = lax.rsqrt(jnp.mean(pre * pre, axis=-1, keepdims=True) + EPSILON)
    embedded = (pre * inverse).astype(jnp.bfloat16)
    similar = jnp.dot(embedded[:query_count], embedded.T, preferred_element_type=jnp.float32)
    factor = SCORE_SCALE / pre.shape[1]
    scores = factor * jnp.take_along_axis(similar, candidates, axis=1)
    perturbed = scores[:, None, :] + perturbation
    highest = jnp.max(perturbed, axis=-1, keepdims=True)
    exponent = jnp.exp(perturbed - highest)
    weights_soft = exponent / jnp.sum(exponent, axis=-1, keepdims=True)
    target = (jnp.arange(candidates.shape[1], dtype=jnp.int32) < TOP).astype(jnp.float32)
    d_scores = LOSS_SCALE * (TOP * jnp.mean(weights_soft, axis=1) - target[None, :])
    query_index = jnp.broadcast_to(
        jnp.arange(query_count, dtype=jnp.int32)[:, None], candidates.shape
    )
    d_similar = (
        jnp.zeros((query_count, embedded.shape[0]), jnp.float32)
        .at[query_index, candidates]
        .add(d_scores)
        .astype(jnp.bfloat16)
    )
    d_embedded = factor * lax.dot_general(
        d_similar,
        embedded[:query_count],
        (((0,), (0,)), ((), ())),
        preferred_element_type=jnp.float32,
    )
    d_queries = factor * jnp.dot(d_similar, embedded, preferred_element_type=jnp.float32)
    d_embedded = d_embedded.at[:query_count].add(d_queries)
    d_pre = inverse * d_embedded - inverse * inverse * inverse * pre * jnp.mean(
        d_embedded * pre, axis=-1, keepdims=True
    )
    return d_pre.astype(jnp.bfloat16)


def body(features, neighbours, send_rows, send_counts, candidates, perturbation, weight):
    feature_rows = features[0]
    neighbour_rows = neighbours[0]
    outgoing_rows = send_rows[0, 0]
    arriving_counts = send_counts[0, 0]
    groups = lax.axis_size("graph")
    capacity = outgoing_rows.shape[1]
    row_count = feature_rows.shape[0]
    feature_width = feature_rows.shape[1]
    fanout = neighbour_rows.shape[1]
    table_rows = row_count + groups * capacity
    outgoing = feature_rows[outgoing_rows.reshape(-1)].reshape(groups, capacity, feature_width)
    arrived = lax.all_to_all(outgoing, "graph", split_axis=0, concat_axis=0, tiled=True)
    keep = jnp.arange(capacity, dtype=jnp.int32)[None, :] < arriving_counts[:, None]
    halo = jnp.where(keep[:, :, None], arrived, jnp.zeros((), jnp.bfloat16)).reshape(
        groups * capacity, feature_width
    )
    table_index = jnp.arange(table_rows, dtype=jnp.int32)
    counted = jnp.zeros((row_count, table_rows), jnp.float32)
    for column in range(fanout):
        counted = counted + (neighbour_rows[:, column][:, None] == table_index[None, :]).astype(
            jnp.float32
        )
    adjacency = counted.astype(jnp.bfloat16)
    start_total = feature_rows.astype(jnp.float32)
    table = jnp.concatenate([feature_rows, halo], axis=0)
    total = start_total + jnp.dot(adjacency, table, preferred_element_type=jnp.float32)
    mean_rows = (total / (fanout + 1)).astype(jnp.bfloat16)
    d_pre = embed_backward(mean_rows, weight, candidates[0], perturbation[0])
    rows_summed = lax.psum_scatter(
        lax.dot_general(
            mean_rows, d_pre, (((0,), (0,)), ((), ())), preferred_element_type=jnp.float32
        ),
        "graph",
        scatter_dimension=0,
        tiled=True,
    )
    weight_tile = lax.psum_scatter(rows_summed, "replica", scatter_dimension=1, tiled=True)
    weight_grad = weight_tile / math.sqrt(groups * lax.axis_size("replica"))
    share = (
        lax.dot_general(d_pre, weight, (((1,), (1,)), ((), ())), preferred_element_type=jnp.float32)
        / (fanout + 1)
    ).astype(jnp.bfloat16)
    d_table = lax.dot_general(
        adjacency, share, (((0,), (0,)), ((), ())), preferred_element_type=jnp.float32
    )
    d_local = share.astype(jnp.float32) + d_table[:row_count]
    halo_grad = jnp.where(keep.reshape(-1)[:, None], d_table[row_count:], 0.0).astype(jnp.bfloat16)
    returned = lax.all_to_all(
        halo_grad.reshape(groups, capacity, feature_width),
        "graph",
        split_axis=0,
        concat_axis=0,
        tiled=True,
    )
    d_rows = d_local.at[outgoing_rows.reshape(-1)].add(
        returned.reshape(groups * capacity, feature_width).astype(jnp.float32)
    )
    return (d_rows.astype(jnp.bfloat16)[None], weight_grad)


def solution(mesh):
    placed = (
        P("replica", "graph", None),
        P("replica", "graph", None),
        P("replica", "graph", None, None),
        P("replica", "graph", None),
        P("replica", "graph", None),
        P("replica", "graph", None, None),
        P(),
    )
    return jax.shard_map(
        body,
        mesh=mesh,
        in_specs=placed,
        out_specs=(P("replica", "graph", None), P("graph", "replica")),
        check_vma=False,
    )
```

profile of v0, /device:TPU:2, one launch (start us, length us, event | category | flops | bytes accessed | tf_op | source)
XLA Modules:
  0.0 602.1 jit_solution(6769162037075862525)
XLA Ops:
  7.2 0.0 copy-start
  7.2 0.0 copy-start.2
  7.2 0.8 copy.11
  8.0 0.1 reshape_squeeze.4
  8.2 0.0 copy-start.4
  8.2 0.0 copy-start.5
  8.2 1.8 gather_fusion
  10.0 0.0 copy-start.6
  10.0 0.0 copy-start.3
  10.1 0.0 copy-start.1
  10.1 0.7 reshape.201
  10.8 29.4 %all-to-all-start = ((bf16[64,2,512]{2,1,0:T(2,128)(2,1)}), bf16[64,2,512]{2,1,0:T(2,128)(2,1)S(1)}, u32[]{:S(2)}, u32[]{:S(2)}) async-start(bf16[64,2,512]{2,1,0:T(2,128)(2,1)} %reshape.201), calls=%async_computation | async-start | bytes 262144 | tf_op jit(solution)/shard_map/all_to_all | solution.py:65
  40.1 0.0 reduce-scatter.5.cloned.1.call-start
  40.2 0.0 copy-done.2
  40.3 0.0 copy-done.4
  40.3 0.1 multiply_reduce_fusion.2
  40.4 0.0 copy-done.5
  40.4 0.1 and_reduce_fusion
  40.5 0.0 copy-done.6
  40.5 0.1 iota_compare_fusion.16
  40.6 0.0 copy-done.3
  40.6 31.3 %all-to-all-done = bf16[64,2,512]{2,1,0:T(2,128)(2,1)S(1)} async-done(((bf16[64,2,512]{2,1,0:T(2,128)(2,1)}), bf16[64,2,512]{2,1,0:T(2,128)(2,1)S(1)}, u32[]{:S(2)}, u32[]{:S(2)}) %all-to-all-start) | async-done | bytes 131104 | tf_op jit(solution)/shard_map/all_to_all | solution.py:65
  72.0 0.2 broadcast_select_fusion
  72.2 0.1 reshape.202
  72.3 0.0 copy-done.1
  72.3 0.5 fusion.6
  72.7 0.0 copy-done
  72.7 0.3 multiply_reduce_fusion.1
  73.1 0.1 multiply_convert_fusion
  73.2 0.1 fusion.17
  73.3 0.0 copy-start.7
  73.3 100.9 %gather_fusion.1 = f32[16384]{0:T(1024)S(1)} fusion(f32[32,128]{1,0:T(8,128)S(1)} %fusion.17, s32[16384]{0:T(1024)S(1)} %bitcast.82), kind=kCustom, calls=%fused_computation.1 | custom fusion | bytes 262144 | tf_op jit(solution)/shard_map/jit(take_along_axis)/gather | solution.py:23
  174.2 0.0 copy-done.7
  174.2 0.3 fusion.29
  174.6 113.5 %scatter_custom_fusion.1 = f32[4096]{0:T(1024)S(1)} fusion(s32[16384]{0:T(1024)S(1)} %bitcast.86, f32[16384]{0:T(1024)S(1)} %bitcast.87, f32[]{:T(128)} %constant.70.clone.1), kind=kCustom, calls=%fused_computation.65 | custom fusion | flops 16384 | bytes 16388
  288.1 0.2 convolution_multiply_fusion.1
  288.3 0.1 fusion.9
  288.5 0.1 multiply_reduce_fusion
  288.6 0.1 subtract_convert_fusion
  288.7 1.3 fusion.30
  290.0 0.0 reduce-scatter.5.cloned.1.call-update
  290.1 0.1 lt.80
  290.2 0.3 fusion.7
  290.5 0.6 fusion.28
  291.1 0.1 fusion.10
  291.2 0.7 reshape.203
  291.9 4.6 all-to-all-start.1
  296.6 0.0 reduce-scatter.7.cloned.1.call-start
  296.6 32.3 %all-to-all-done.1 = bf16[64,2,512]{2,1,0:T(2,128)(2,1)S(1)} async-done(((bf16[64,2,512]{2,1,0:T(2,128)(2,1)}), bf16[64,2,512]{2,1,0:T(2,128)(2,1)S(1)}, u32[]{:S(2)}, u32[]{:S(2)}) %all-to-all-start.1) | async-done | bytes 131104 | tf_op jit(solution)/shard_map/all_to_all | solution.py:101
  328.9 1.5 scatter_fusion
  330.4 151.8 %reduce-scatter.5.cloned.1.call-done = f32[8,512]{1,0:T(8,128)} async-done(((f32[512,512]{1,0:T(8,128)}), f32[8,512]{1,0:T(8,128)}) %reduce-scatter.5.cloned.1.call-update) | async-done | bytes 16400 | tf_op jit(solution)/shard_map/reduce_scatter | solution.py:82
  482.2 1.5 copy.12
  483.8 0.0 reduce-scatter.7.cloned.1.call-update
  483.8 0.7 convert_bitcast_fusion
  484.5 109.4 %reduce-scatter.7.cloned.1.call-done = f32[32,8]{1,0:T(8,128)} async-done(((f32[512,8]{1,0:T(8,128)}), f32[32,8]{1,0:T(8,128)}) %reduce-scatter.7.cloned.1.call-update) | async-done | bytes 1040
  593.9 0.8 copy.13
  594.7 0.6 broadcast_multiply_fusion
  (17 shorter events, 0.3 us)
Async XLA Ops:
  7.2 65.6 %copy-start = (bf16[512,512]{1,0:T(8,128)(2,1)S(1)}, bf16[512,512]{1,0:T(8,128)(2,1)}, u32[]{:S(2)}) copy-start(bf16[512,512]{1,0:T(8,128)(2,1)} %param.15) | copy-start | bytes 1572868
  7.2 33.0 %copy-start.2 = (s32[1,32,512]{2,1,0:T(8,128)S(1)}, s32[1,32,512]{2,1,0:T(8,128)}, u32[]{:S(2)}) copy-start(s32[1,32,512]{2,1,0:T(8,128)} %param.13) | copy-start | bytes 196612
  8.2 32.1 %copy-start.4 = (s32[2]{0:T(128)S(1)}, s32[2]{0:T(128)}, u32[]{:S(2)}) copy-start(s32[2]{0:T(128)} %constant.86) | copy-start | bytes 28
  8.2 32.2 %copy-start.5 = (s32[2]{0:T(128)S(1)}, s32[2]{0:T(128)}, u32[]{:S(2)}) copy-start(s32[2]{0:T(128)} %constant.89) | copy-start | bytes 28
  10.0 30.5 %copy-start.6 = (s32[1,1,64]{2,1,0:T(1,128)S(1)}, s32[1,1,64]{2,1,0:T(1,128)}, u32[]{:S(2)}) copy-start(s32[1,1,64]{2,1,0:T(1,128)} %param.12) | copy-start | bytes 772
  10.0 30.6 %copy-start.3 = (s32[1,128,16]{1,2,0:T(8,128)S(1)}, s32[1,128,16]{1,2,0:T(8,128)}, u32[]{:S(2)}) copy-start(s32[1,128,16]{1,2,0:T(8,128)} %param.10) | copy-start | bytes 24580
  10.1 62.2 %copy-start.1 = (bf16[1,128,512]{2,1,0:T(8,128)(2,1)S(1)}, bf16[1,128,512]{2,1,0:T(8,128)(2,1)}, u32[]{:S(2)}) copy-start(bf16[1,128,512]{2,1,0:T(8,128)(2,1)} %param.9) | copy-start | bytes 393220
  10.8 61.2 %all-to-all-start = ((bf16[64,2,512]{2,1,0:T(2,128)(2,1)}), bf16[64,2,512]{2,1,0:T(2,128)(2,1)S(1)}, u32[]{:S(2)}, u32[]{:S(2)}) async-start(bf16[64,2,512]{2,1,0:T(2,128)(2,1)} %reshape.201), calls=%async_computation | async-start | bytes 262144 | tf_op jit(solution)/shard_map/all_to_all | solution.py:65
  40.1 442.1 %reduce-scatter.5.cloned.1.call-start = ((), (), s32[]{:S(2)}) async-start(), calls=%async_computation.4 | async-start | bytes 1064960 | tf_op jit(solution)/shard_map/reduce_scatter | solution.py:82
  73.3 100.9 %copy-start.7 = (f32[1,32,4,512]{3,2,1,0:T(4,128)S(1)}, f32[1,32,4,512]{3,2,1,0:T(4,128)}, u32[]{:S(2)}) copy-start(f32[1,32,4,512]{3,2,1,0:T(4,128)} %param.14) | copy-start | bytes 786436
  291.9 37.0 %all-to-all-start.1 = ((bf16[64,2,512]{2,1,0:T(2,128)(2,1)}), bf16[64,2,512]{2,1,0:T(2,128)(2,1)S(1)}, u32[]{:S(2)}, u32[]{:S(2)}) async-start(bf16[64,2,512]{2,1,0:T(2,128)(2,1)} %reshape.203), calls=%async_computation.1 | async-start | bytes 262144 | tf_op jit(solution)/shard_map/all_to_all | solution.py:101
  296.6 297.3 %reduce-scatter.7.cloned.1.call-start = ((), (), s32[]{:S(2)}) async-start(), calls=%async_computation.5 | async-start | bytes 278528
Sparse Core Ops, SparseCore 0:
  290.2 192.0 reduce-scatter.4
  488.3 105.5 reduce-scatter.6
where the time goes:
time: 603 us; the launch traced here: 602 us
  waiting for transfers between devices  325 us (54%)
  other arithmetic  118 us (20%)
  local copies, waits for them, and re-layouts  108 us (18%)
  starting transfers between devices  34.1 us (6%)
  between operations  14.4 us (2%)
    reduce_scatter x1, waiting for transfers between devices, body(): lax.psum_scatter(lax.dot_general(mean_rows, d_pre, (((0,), (0,)), ((), ()...  152 us
    unnamed x6, other arithmetic  114 us
    unnamed x3, waiting for transfers between devices  109 us
    gather x2, local copies, waits for them, and re-layouts, embed_backward(): scores = factor * jnp.take_along_axis(similar, candidates, axis=1)  101 us
    all_to_all x1, waiting for transfers between devices, body(): lax.all_to_all(halo_grad.reshape(groups, capacity, feature_width), 'graph...  32.3 us
    all_to_all x1, waiting for transfers between devices, body(): lax.all_to_all(outgoing, 'graph', split_axis=0, concat_axis=0, tiled=True)  31.3 us
    all_to_all x1, starting transfers between devices, body(): lax.all_to_all(outgoing, 'graph', split_axis=0, concat_axis=0, tiled=True)  29.4 us
  transfers between devices with their start and end apart: 4, of which 4 were waited for; matrix products, arithmetic and copies ran while one was open for 1% of the time, Pallas kernels for 0%

commit v1 on v0

v1 whole, which is shorter than its diff:
```python
import functools
import math

import jax
import jax.numpy as jnp
from jax import lax
from jax.experimental import pallas as pl
from jax.experimental.pallas import tpu as pltpu
from jax.sharding import PartitionSpec as P

TOP = 20
SCORE_SCALE = 16.0
LOSS_SCALE = 16.0
EPSILON = 1e-05
LANES = 128
MESH = pl.DeviceIdType.MESH
F32 = jnp.float32
BF16 = jnp.bfloat16


def iota(shape, axis):
    return lax.broadcasted_iota(jnp.int32, shape, axis)


def one_hot(mask):
    return jnp.where(mask, 1.0, 0.0).astype(BF16)


def dot(a, b, a_axis=1, b_axis=0):
    return lax.dot_general(
        a, b, (((a_axis,), (b_axis,)), ((), ())), preferred_element_type=F32
    )


def wait_all(ref, sem, count):
    part = ref.at[pl.ds(0, count)]
    pltpu.make_async_copy(part, part, sem).wait()


def kernel(
    groups,
    replicas,
    features,
    neighbours,
    send_rows,
    counts,
    candidates,
    perturbation,
    weight,
    d_features,
    weight_grad,
    stage,
    out_send,
    out_recv,
    ret_send,
    ret_recv,
    mean_send,
    mean_recv,
    dpre_send,
    dpre_recv,
    tile_send,
    tile_recv,
    z_send,
    z_recv,
    adj,
    adj_t,
    picks,
    noise,
    total,
    send_sems,
    recv_sems,
):
    mg = lax.axis_index("graph")
    mr = lax.axis_index("replica")
    core = lax.rem(mg, 2)
    chip = lax.div(mg, 2)
    chips = groups // 2
    partner = chip * 2 + 1 - core
    rows, width = features.shape
    fanout = neighbours.shape[0]
    capacity = send_rows.shape[0]
    queries, cands = candidates.shape
    samples = perturbation.shape[1]
    blocks = width // LANES
    parts = capacity * blocks
    slots = groups * capacity
    tall, wide = weight_grad.shape
    half = tall * chips

    barrier = pltpu.get_barrier_semaphore()

    def greet_graph(i, carry):
        pl.semaphore_signal(
            barrier, inc=1, device_id=(lax.rem(mg + i, groups), mr), device_id_type=MESH
        )
        return carry

    def greet_replica(i, carry):
        pl.semaphore_signal(
            barrier, inc=1, device_id=(mg, lax.rem(mr + i, replicas)), device_id_type=MESH
        )
        return carry

    lax.fori_loop(1, groups, greet_graph, 0)
    lax.fori_loop(1, replicas, greet_replica, 0)

    def far_first(i):
        step = lax.div(i + 1, 2)
        sign = 1 - 2 * lax.rem(i, 2)
        return lax.rem(mg + groups // 2 + sign * step + groups, groups)

    def send_all(source, target, slot):
        def step(i, carry):
            peer = far_first(i)
            pltpu.make_async_remote_copy(
                src_ref=source.at[peer],
                dst_ref=target.at[mg],
                send_sem=send_sems.at[slot],
                recv_sem=recv_sems.at[slot],
                device_id=(peer, mr),
                device_id_type=MESH,
            ).start()
            return carry

        lax.fori_loop(0, groups - 1, step, 0)

    def pack(values, target):
        for k in range(capacity):
            for j in range(blocks):
                stage[pl.ds(k * blocks + j, groups, stride=parts), :] = values[
                    k * groups : (k + 1) * groups, j * LANES : (j + 1) * LANES
                ]
        target[...] = stage[...].reshape(groups, parts, LANES).astype(BF16)

    def unpack(source):
        stage[...] = source[...].astype(F32).reshape(groups * parts, LANES)
        return jnp.concatenate(
            [
                jnp.concatenate(
                    [
                        stage[pl.ds(k * blocks + j, groups, stride=parts), :]
                        for j in range(blocks)
                    ],
                    axis=1,
                )
                for k in range(capacity)
            ],
            axis=0,
        ).astype(BF16)

    feature_rows = features[...]
    row_of = iota((rows, groups), 0)
    sent = [one_hot(row_of == send_rows[k : k + 1, :]) for k in range(capacity)]
    pack(
        jnp.concatenate([dot(s, feature_rows, 0, 0) for s in sent], axis=0), out_send
    )
    out_recv[mg] = out_send[mg]

    pl.semaphore_wait(barrier, groups + replicas - 2)
    send_all(out_send, out_recv, 0)

    table = rows + slots
    place = iota((table, rows), 0)
    past = place - rows
    slot_id = rows + capacity * lax.rem(past, groups) + lax.div(past, groups)
    name = jnp.where(past < 0, place, slot_id)
    counted = jnp.zeros((table, rows), F32)
    for f in range(fanout):
        counted = counted + jnp.where(neighbours[f : f + 1, :] == name, 1.0, 0.0)
    count_column = jnp.sum(
        jnp.where(iota((groups, groups), 0) == iota((groups, groups), 1), counts[...], 0),
        axis=1,
        keepdims=True,
    )
    keep = jnp.concatenate(
        [jnp.ones((rows, 1), F32)]
        + [jnp.where(count_column > k, 1.0, 0.0) for k in range(capacity)],
        axis=0,
    )
    counted = counted * keep
    adj_t[...] = counted.astype(BF16)
    adj[...] = counted.T.astype(BF16)
    node = iota((rows, cands), 0)

    def pick(q, carry):
        picks[pl.ds(pl.multiple_of(q * rows, rows), rows), :] = one_hot(
            candidates[pl.ds(q, 1), :] == node
        )
        return carry

    lax.fori_loop(0, queries, pick, 0)
    for m in range(samples):
        noise[m] = perturbation[:, m, :]
    total[...] = feature_rows.astype(F32) + dot(adj[:, :rows], feature_rows)
    column = iota((width, half), 0)
    order = iota((width, half), 1)
    wanted = (lax.rem(order, chips) * 2) * tall + lax.div(order, chips)
    mine = one_hot(column == wanted + core * tall)
    theirs = one_hot(column == wanted + (1 - core) * tall)

    wait_all(out_recv, recv_sems.at[0], groups - 1)
    halo = unpack(out_recv)
    scale = 1.0 / (fanout + 1)
    mean_rows = ((total[...] + dot(adj[:, rows:], halo)) * scale).astype(BF16)
    pre = dot(mean_rows, weight[...])
    inverse = lax.rsqrt(jnp.mean(pre * pre, axis=-1, keepdims=True) + EPSILON)
    embedded = (pre * inverse).astype(BF16)

    def to_partner(source, target, slot):
        return pltpu.make_async_remote_copy(
            src_ref=source,
            dst_ref=target,
            send_sem=send_sems.at[slot],
            recv_sem=recv_sems.at[slot],
            device_id=(partner, mr),
            device_id_type=MESH,
        )

    mean_send[...] = dot(mean_rows, theirs).astype(BF16)
    mean_copy = to_partner(mean_send, mean_recv, 1)
    mean_copy.start()
    mean_mine = dot(mean_rows, mine).astype(BF16)

    factor = SCORE_SCALE / width
    similar = factor * dot(embedded[:queries], embedded, 1, 1)
    scores = jnp.concatenate(
        [
            jnp.take_along_axis(
                similar,
                candidates[:, c * rows : (c + 1) * rows],
                axis=1,
                mode="promise_in_bounds",
            )
            for c in range(cands // rows)
        ],
        axis=1,
    )
    soft = jnp.zeros((queries, cands), F32)
    for m in range(samples):
        shifted = scores + noise[m]
        exponent = jnp.exp(shifted - jnp.max(shifted, axis=-1, keepdims=True))
        soft = soft + exponent * (1.0 / jnp.sum(exponent, axis=-1, keepdims=True))
    engaged = jnp.where(iota((queries, cands), 1) < TOP, LOSS_SCALE, 0.0)
    d_scores = (LOSS_SCALE * TOP / samples) * soft - engaged
    high = d_scores.astype(BF16)
    low = (d_scores - high.astype(F32)).astype(BF16)
    both = jnp.concatenate(
        [high, low, jnp.zeros((LANES - 2 * queries, cands), BF16)], axis=0
    )
    lane = iota((rows, LANES), 1)
    spread = jnp.zeros((rows, LANES), F32)
    group = 8
    for g in range(queries // group):
        some = dot(picks[g * group * rows : (g + 1) * group * rows, :], both, 1, 1)
        for i in range(group):
            q = g * group + i
            spread = spread + jnp.where(
                lax.rem(lane, queries) == q, some[i * rows : (i + 1) * rows, :], 0.0
            )
    spread = spread + pltpu.roll(spread, LANES - queries, axis=1)
    similar_t = jnp.where(lane < queries, spread, 0.0).astype(BF16).astype(F32)
    mixed = jnp.concatenate([similar_t, similar_t.T], axis=1).astype(BF16)
    d_embedded = factor * dot(mixed, jnp.concatenate([embedded, embedded], axis=0))
    slope = jnp.mean(d_embedded * pre, axis=-1, keepdims=True)
    d_pre = (inverse * d_embedded - inverse * inverse * inverse * pre * slope).astype(BF16)
    dpre_send[...] = d_pre
    dpre_copy = to_partner(dpre_send, dpre_recv, 2)
    dpre_copy.start()

    share = (dot(d_pre, weight[...], 1, 1) * scale).astype(BF16)
    pack(dot(adj_t[rows:, :], share), ret_send)
    ret_recv[mg] = ret_send[mg]
    send_all(ret_send, ret_recv, 3)
    total[...] = share.astype(F32) + dot(adj_t[:rows, :], share)

    mean_copy.wait()
    dpre_copy.wait()
    product = dot(d_pre, mean_mine, 0, 0) + dot(dpre_recv[...], mean_recv[...], 0, 0)
    tile_send[...] = product.astype(BF16).reshape(replicas, wide, half)
    tile_recv[mr] = tile_send[mr]

    def send_tile(i, carry):
        peer = lax.rem(mr + i, replicas)
        pltpu.make_async_remote_copy(
            src_ref=tile_send.at[peer],
            dst_ref=tile_recv.at[mr],
            send_sem=send_sems.at[4],
            recv_sem=recv_sems.at[4],
            device_id=(mg, peer),
            device_id_type=MESH,
        ).start()
        return carry

    lax.fori_loop(1, replicas, send_tile, 0)
    wait_all(tile_recv, recv_sems.at[4], replicas - 1)
    plane = tile_recv[0].astype(F32)
    for p in range(1, replicas):
        plane = plane + tile_recv[p].astype(F32)
    if wide < LANES:
        plane = jnp.concatenate([plane, jnp.zeros((LANES - wide, half), F32)], axis=0)
    plane_t = plane.T
    per = LANES // wide
    for h in range(tall // per):
        packed = plane_t[h * per * chips : (h * per + 1) * chips, :]
        for i in range(1, per):
            e = h * per + i
            packed = packed + pltpu.roll(
                plane_t[e * chips : (e + 1) * chips, :], i * wide, axis=1
            )
        for c in range(chips):
            z_send[c, h : h + 1, :] = packed[c : c + 1, :]
    z_recv[chip] = z_send[chip]

    def send_z(i, carry):
        peer = lax.rem(chip + i, chips)
        pltpu.make_async_remote_copy(
            src_ref=z_send.at[peer],
            dst_ref=z_recv.at[chip],
            send_sem=send_sems.at[5],
            recv_sem=recv_sems.at[5],
            device_id=(peer * 2 + core, mr),
            device_id_type=MESH,
        ).start()
        return carry

    lax.fori_loop(1, chips, send_z, 0)

    wait_all(ret_recv, recv_sems.at[3], groups - 1)
    returned = unpack(ret_recv)
    d_rows = total[...]
    for k in range(capacity):
        d_rows = d_rows + dot(sent[k], returned[k * groups : (k + 1) * groups, :])
    d_features[...] = d_rows.astype(BF16)

    wait_all(z_recv, recv_sems.at[5], chips - 1)
    block = jnp.sum(z_recv[...], axis=0) * (1.0 / math.sqrt(groups * replicas))
    for e in range(tall):
        line = block[e // per : e // per + 1, :]
        if e % per:
            line = pltpu.roll(line, LANES - (e % per) * wide, axis=1)
        weight_grad[e : e + 1, :] = line[:, :wide]

    wait_all(out_send, send_sems.at[0], groups - 1)
    wait_all(ret_send, send_sems.at[3], groups - 1)
    wait_all(tile_send, send_sems.at[4], replicas - 1)
    wait_all(z_send, send_sems.at[5], chips - 1)


def body(
    groups, replicas, features, neighbours, send_rows, send_counts, candidates, perturbation, weight
):
    rows, width = features.shape[1:]
    capacity = send_rows.shape[3]
    queries, cands = candidates.shape[1:]
    samples = perturbation.shape[2]
    slots = groups * capacity
    parts = capacity * width // LANES
    tall, wide = width // groups, width // replicas
    chips = groups // 2
    half = tall * chips
    packed = tall * wide // LANES
    vmem = pl.BlockSpec(memory_space=pltpu.VMEM)
    message = pltpu.VMEM((groups, parts, LANES), BF16)
    d_features, weight_grad = pl.pallas_call(
        functools.partial(kernel, groups, replicas),
        name="layer",
        out_shape=(
            jax.ShapeDtypeStruct((rows, width), BF16),
            jax.ShapeDtypeStruct((tall, wide), F32),
        ),
        in_specs=[vmem] * 7,
        out_specs=(vmem, vmem),
        scratch_shapes=[
            pltpu.VMEM((groups * parts, LANES), F32),
            message,
            message,
            message,
            message,
            pltpu.VMEM((rows, half), BF16),
            pltpu.VMEM((rows, half), BF16),
            pltpu.VMEM((rows, width), BF16),
            pltpu.VMEM((rows, width), BF16),
            pltpu.VMEM((replicas, wide, half), BF16),
            pltpu.VMEM((replicas, wide, half), BF16),
            pltpu.VMEM((chips, packed, LANES), F32),
            pltpu.VMEM((chips, packed, LANES), F32),
            pltpu.VMEM((rows, rows + slots), BF16),
            pltpu.VMEM((rows + slots, rows), BF16),
            pltpu.VMEM((queries * rows, cands), BF16),
            pltpu.VMEM((samples, queries, cands), F32),
            pltpu.VMEM((rows, width), F32),
            pltpu.SemaphoreType.DMA((6,)),
            pltpu.SemaphoreType.DMA((6,)),
        ],
        compiler_params=pltpu.CompilerParams(
            collective_id=0, has_side_effects=True, vmem_limit_bytes=40 * 1024 * 1024
        ),
    )(
        features[0],
        neighbours[0].T,
        send_rows[0, 0].T,
        send_counts[0],
        candidates[0],
        perturbation[0],
        weight,
    )
    return d_features[None], weight_grad


def solution(mesh):
    placed = (
        P("replica", "graph", None),
        P("replica", "graph", None),
        P("replica", "graph", None, None),
        P("replica", "graph", None),
        P("replica", "graph", None),
        P("replica", "graph", None, None),
        P(),
    )
    return jax.shard_map(
        functools.partial(body, mesh.shape["graph"], mesh.shape["replica"]),
        mesh=mesh,
        in_specs=placed,
        out_specs=(P("replica", "graph", None), P("graph", "replica")),
        check_vma=False,
    )
```

time: 603 us -> 77.5 us (0.13)
  the two profiles are of different devices: /device:TPU:2 before, /device:TPU:1 now
where the time goes in v1:
time: 77.5 us; the launch traced here: 77.2 us
  Pallas kernels  70.8 us (91%)
  local copies, waits for them, and re-layouts  5.66 us (7%)
    pallas_call x1, Pallas kernels, body(): pl.pallas_call(functools.partial(kernel, groups, replicas), name='layer',...  70.8 us
    unnamed x16, local copies, waits for them, and re-layouts  5.66 us

profile of v1, /device:TPU:1, one launch (start us, length us, event | category | flops | bytes accessed | tf_op | source)
XLA Modules:
  0.0 77.2 jit_solution(9530380018223173667)
XLA Ops:
  0.6 0.0 copy-start.4
  0.6 0.0 copy-start.5
  0.7 0.0 copy-start.6
  0.7 0.7 copy-done.4
  1.3 0.0 copy-done.5
  1.3 0.0 copy-done.6
  1.3 0.0 copy-start
  1.3 1.0 %copy-done = bf16[512,512]{1,0:T(8,128)(2,1)S(1)} copy-done((bf16[512,512]{1,0:T(8,128)(2,1)S(1)}, bf16[512,512]{1,0:T(8,128)(2,1)}, u32[]{:S(2)}) %copy-start) | copy-done | bytes 524312
  2.4 0.0 copy-start.1
  2.4 0.9 %copy-done.1 = f32[1,32,4,512]{3,2,1,0:T(4,128)S(1)} copy-done((f32[1,32,4,512]{3,2,1,0:T(4,128)S(1)}, f32[1,32,4,512]{3,2,1,0:T(4,128)}, u32[]{:S(2)}) %copy-start.1) | copy-done | bytes 262168
  3.3 0.0 copy-start.2
  3.3 0.9 %copy-done.2 = bf16[1,128,512]{2,1,0:T(8,128)(2,1)S(1)} copy-done((bf16[1,128,512]{2,1,0:T(8,128)(2,1)S(1)}, bf16[1,128,512]{2,1,0:T(8,128)(2,1)}, u32[]{:S(2)}) %copy-start.2) | copy-done | bytes 131096
  4.2 0.0 copy-start.3
  4.2 0.8 %copy-done.3 = s32[1,32,512]{2,1,0:T(8,128)S(1)} copy-done((s32[1,32,512]{2,1,0:T(8,128)S(1)}, s32[1,32,512]{2,1,0:T(8,128)}, u32[]{:S(2)}) %copy-start.3) | copy-done | bytes 65560
  5.1 70.8 %layer.1 = (bf16[128,512]{1,0:T(8,128)(2,1)S(1)}, f32[8,32]{1,0:T(8,128)S(1)}) custom-call(bf16[128,512]{1,0:T(8,128)(2,1)S(1)} %bitcast.12, s32[16,128]{1,0:T(8,128)S(1)} %bitcast.15, s32[2,64]{1,0:T(2,128)S(1)} %bitcast.16, s32[1,64]{1,0:T(1,128)S(1)} %bitcast.17, s32[32,512]{1,0:T(8,128)S(1)} %bitcast.14, f32[32,4,512]{2,1,0:T(4,128)S(1)} %bitcast.11, ...), custom_call_target="tpu_custom_call" | custom-call | tf_op jit(solution)/shard_map/layer/pallas_call | solution.py:364
  75.9 0.7 copy.11
  76.6 0.6 copy.12
Async XLA Ops:
  0.6 0.7 copy-start.4
  0.6 0.7 copy-start.5
  0.7 0.7 copy-start.6
  1.3 1.0 %copy-start = (bf16[512,512]{1,0:T(8,128)(2,1)S(1)}, bf16[512,512]{1,0:T(8,128)(2,1)}, u32[]{:S(2)}) copy-start(bf16[512,512]{1,0:T(8,128)(2,1)} %weight.1) | copy-start | bytes 1572868
  2.4 0.9 %copy-start.1 = (f32[1,32,4,512]{3,2,1,0:T(4,128)S(1)}, f32[1,32,4,512]{3,2,1,0:T(4,128)}, u32[]{:S(2)}) copy-start(f32[1,32,4,512]{3,2,1,0:T(4,128)} %param.12) | copy-start | bytes 786436
  3.3 0.9 %copy-start.2 = (bf16[1,128,512]{2,1,0:T(8,128)(2,1)S(1)}, bf16[1,128,512]{2,1,0:T(8,128)(2,1)}, u32[]{:S(2)}) copy-start(bf16[1,128,512]{2,1,0:T(8,128)(2,1)} %param.7) | copy-start | bytes 393220
  4.2 0.8 %copy-start.3 = (s32[1,32,512]{2,1,0:T(8,128)S(1)}, s32[1,32,512]{2,1,0:T(8,128)}, u32[]{:S(2)}) copy-start(s32[1,32,512]{2,1,0:T(8,128)} %param.11) | copy-start | bytes 196612

commit v2 on v1

v2 whole, which is shorter than its diff:
```python
import functools
import math

import jax
import jax.numpy as jnp
from jax import lax
from jax.experimental import pallas as pl
from jax.experimental.pallas import tpu as pltpu
from jax.sharding import PartitionSpec as P

TOP = 20
SCORE_SCALE = 16.0
LOSS_SCALE = 16.0
EPSILON = 1e-05
LANES = 128
MESH = pl.DeviceIdType.MESH
F32 = jnp.float32
BF16 = jnp.bfloat16


def iota(shape, axis):
    return lax.broadcasted_iota(jnp.int32, shape, axis)


def one_hot(mask):
    return jnp.where(mask, 1.0, 0.0).astype(BF16)


def dot(a, b, a_axis=1, b_axis=0):
    return lax.dot_general(
        a, b, (((a_axis,), (b_axis,)), ((), ())), preferred_element_type=F32
    )


def wait_all(ref, sem, count):
    part = ref.at[pl.ds(0, count)]
    pltpu.make_async_copy(part, part, sem).wait()


def kernel(
    groups,
    replicas,
    features,
    neighbours,
    send_rows,
    counts,
    candidates,
    perturbation,
    weight,
    d_features,
    weight_grad,
    feature_buf,
    neighbour_buf,
    row_buf,
    count_buf,
    candidate_buf,
    noise_buf,
    weight_buf,
    stage,
    out_send,
    out_recv,
    relay,
    ret_send,
    ret_recv,
    mean_send,
    mean_recv,
    dpre_send,
    dpre_recv,
    tile_send,
    tile_recv,
    z_send,
    z_recv,
    adj,
    adj_t,
    picks,
    noise,
    total,
    send_sems,
    recv_sems,
    load_sems,
    relay_sems,
):
    mg = lax.axis_index("graph")
    mr = lax.axis_index("replica")
    core = lax.rem(mg, 2)
    chip = lax.div(mg, 2)
    chips = groups // 2
    partner = chip * 2 + 1 - core
    rows, width = features.shape
    fanout = neighbours.shape[0]
    capacity = send_rows.shape[0]
    queries, cands = candidates.shape
    samples = perturbation.shape[1]
    blocks = width // LANES
    parts = capacity * blocks
    slots = groups * capacity
    tall, wide = weight_grad.shape
    half = tall * chips

    near = chips // 4

    barrier = pltpu.get_barrier_semaphore()

    def greet(g, r):
        pl.semaphore_signal(barrier, inc=1, device_id=(g, r), device_id_type=MESH)

    def beside(i):
        return lax.rem(2 * chip + i, groups)

    def greet_near(i, carry):
        greet(beside(2 * near + 1 - i), mr)
        greet(beside(groups - 2 * near + i), mr)
        return carry

    def greet_replica(i, carry):
        greet(mg, lax.rem(mr + i, replicas))
        return carry

    lax.fori_loop(0, 2 * near, greet_near, 0)
    greet(partner, mr)
    lax.fori_loop(1, replicas, greet_replica, 0)

    loads = [
        pltpu.make_async_copy(source, target, load_sems.at[n])
        for n, (source, target) in enumerate(
            (
                (features, feature_buf),
                (send_rows, row_buf),
                (neighbours, neighbour_buf),
                (counts, count_buf),
                (candidates, candidate_buf),
                (perturbation, noise_buf),
                (weight, weight_buf),
            )
        )
    ]
    for load in loads:
        load.start()

    def remote(source, target, slot, g, r):
        return pltpu.make_async_remote_copy(
            src_ref=source,
            dst_ref=target,
            send_sem=send_sems.at[slot],
            recv_sem=recv_sems.at[slot],
            device_id=(g, r),
            device_id_type=MESH,
        )

    def line_up(i):
        return jnp.where(i < chips // 2, i, chips + chips // 2 - 1 - i)

    def pack(values, target):
        for k in range(capacity):
            for j in range(blocks):
                stage[pl.ds(k * blocks + j, groups, stride=parts), :] = values[
                    k * groups : (k + 1) * groups, j * LANES : (j + 1) * LANES
                ]
        target[0:groups] = stage[...].reshape(groups, parts, LANES).astype(BF16)

    def unpack(source):
        stage[...] = source[...].astype(F32).reshape(groups * parts, LANES)
        return jnp.concatenate(
            [
                jnp.concatenate(
                    [
                        stage[pl.ds(k * blocks + j, groups, stride=parts), :]
                        for j in range(blocks)
                    ],
                    axis=1,
                )
                for k in range(capacity)
            ],
            axis=0,
        ).astype(BF16)

    loads[0].wait()
    loads[1].wait()
    feature_rows = feature_buf[...]
    row_of = iota((rows, groups), 0)
    sent = [one_hot(row_of == row_buf[k : k + 1, :]) for k in range(capacity)]
    pack(
        jnp.concatenate([dot(s, feature_rows, 0, 0) for s in sent], axis=0), out_send
    )
    out_send[groups : 2 * groups] = out_send[0:groups]
    out_recv[mg] = out_send[mg]

    loads[2].wait()
    loads[3].wait()
    table = rows + slots
    place = iota((table, rows), 0)
    past = place - rows
    slot_id = rows + capacity * lax.rem(past, groups) + lax.div(past, groups)
    name = jnp.where(past < 0, place, slot_id)
    counted = jnp.zeros((table, rows), F32)
    for f in range(fanout):
        counted = counted + jnp.where(neighbour_buf[f : f + 1, :] == name, 1.0, 0.0)
    count_column = jnp.sum(
        jnp.where(iota((groups, groups), 0) == iota((groups, groups), 1), count_buf[...], 0),
        axis=1,
        keepdims=True,
    )
    keep = jnp.concatenate(
        [jnp.ones((rows, 1), F32)]
        + [jnp.where(count_column > k, 1.0, 0.0) for k in range(capacity)],
        axis=0,
    )
    counted = counted * keep
    adj_t[...] = counted.astype(BF16)
    adj[...] = counted.T.astype(BF16)
    loads[4].wait()
    node = iota((rows, cands), 0)

    def pick(q, carry):
        picks[pl.ds(pl.multiple_of(q * rows, rows), rows), :] = one_hot(
            candidate_buf[pl.ds(q, 1), :] == node
        )
        return carry

    lax.fori_loop(0, queries, pick, 0)
    loads[5].wait()
    for m in range(samples):
        noise[m] = noise_buf[:, m, :]
    total[...] = feature_rows.astype(F32) + dot(adj[:, :rows], feature_rows)
    column = iota((width, half), 0)
    order = iota((width, half), 1)
    wing = chips // 2
    lanes = tall * wing
    wanted = (lax.div(order, lanes) * wing + lax.rem(order, wing)) * 2 * tall + lax.rem(
        lax.div(order, wing), tall
    )
    mine = one_hot(column == wanted + core * tall)
    theirs = one_hot(column == wanted + (1 - core) * tall)

    loads[6].wait()

    pl.semaphore_wait(barrier, 4 * near + replicas)
    after, before = beside(2 * near + core), beside(groups - 2 * near + core)

    def relayed(side, k, first, count):
        return relay.at[side, pl.ds(2 * (k - near - 1) + first, count)]

    def launch(side, k, first=0, count=2):
        row = 2 * k if side == 0 else groups - 2 * k
        pltpu.make_async_remote_copy(
            src_ref=out_send.at[pl.ds(2 * chip + row + first, count)],
            dst_ref=relayed(side, k, first, count),
            send_sem=send_sems.at[7],
            recv_sem=relay_sems.at[side, k - near - 1],
            device_id=(after if side == 0 else before, mr),
            device_id_type=MESH,
        ).start()

    def forward(side, k, first=0, count=2):
        part = relayed(side, k, first, count)
        pltpu.make_async_copy(part, part, relay_sems.at[side, k - near - 1]).wait()
        place = 2 * (k - near) if side == 0 else groups - 2 * (k - near)
        source = before if side == 0 else after
        for c in range(first, first + count):
            remote(
                relay.at[side, 2 * (k - near - 1) + c],
                out_recv.at[source],
                0,
                beside(place + c),
                mr,
            ).start()

    def farther(step):
        step(0, 2 * near, 0, 1)
        step(1, 2 * near, 1, 1)

        def both(i, carry):
            step(0, 2 * near - 1 - i)
            step(1, 2 * near - 1 - i)
            return carry

        lax.fori_loop(0, near - 1, both, 0)

    def direct(i):
        remote(out_send.at[2 * chip + i], out_recv.at[mg], 0, beside(i), mr).start()

    def send_near(i, carry):
        direct(2 * near + 1 - i)
        direct(groups - 2 * near + i)
        return carry

    farther(launch)
    lax.fori_loop(0, near, send_near, 0)
    direct(1 - core)
    farther(forward)
    lax.fori_loop(near, 2 * near, send_near, 0)

    wait_all(out_recv, recv_sems.at[0], groups - 1)
    halo = unpack(out_recv)
    scale = 1.0 / (fanout + 1)
    mean_rows = ((total[...] + dot(adj[:, rows:], halo)) * scale).astype(BF16)
    pre = dot(mean_rows, weight_buf[...])
    inverse = lax.rsqrt(jnp.mean(pre * pre, axis=-1, keepdims=True) + EPSILON)
    embedded = (pre * inverse).astype(BF16)

    mean_send[...] = dot(mean_rows, theirs).astype(BF16)
    mean_copy = remote(mean_send, mean_recv, 1, partner, mr)
    mean_copy.start()
    mean_mine = dot(mean_rows, mine).astype(BF16)

    factor = SCORE_SCALE / width
    similar = factor * dot(embedded[:queries], embedded, 1, 1)
    scores = jnp.concatenate(
        [
            jnp.take_along_axis(
                similar,
                candidate_buf[:, c * rows : (c + 1) * rows],
                axis=1,
                mode="promise_in_bounds",
            )
            for c in range(cands // rows)
        ],
        axis=1,
    )
    soft = jnp.zeros((queries, cands), F32)
    for m in range(samples):
        shifted = scores + noise[m]
        exponent = jnp.exp(shifted - jnp.max(shifted, axis=-1, keepdims=True))
        soft = soft + exponent * (1.0 / jnp.sum(exponent, axis=-1, keepdims=True))
    engaged = jnp.where(iota((queries, cands), 1) < TOP, LOSS_SCALE, 0.0)
    d_scores = (LOSS_SCALE * TOP / samples) * soft - engaged
    high = d_scores.astype(BF16)
    low = (d_scores - high.astype(F32)).astype(BF16)
    both = jnp.concatenate(
        [high, low, jnp.zeros((LANES - 2 * queries, cands), BF16)], axis=0
    )
    lane = iota((rows, LANES), 1)
    spread = jnp.zeros((rows, LANES), F32)
    group = 8
    for g in range(queries // group):
        some = dot(picks[g * group * rows : (g + 1) * group * rows, :], both, 1, 1)
        for i in range(group):
            q = g * group + i
            spread = spread + jnp.where(
                lax.rem(lane, queries) == q, some[i * rows : (i + 1) * rows, :], 0.0
            )
    spread = spread + pltpu.roll(spread, LANES - queries, axis=1)
    similar_t = jnp.where(lane < queries, spread, 0.0).astype(BF16).astype(F32)
    mixed = jnp.concatenate([similar_t, similar_t.T], axis=1).astype(BF16)
    d_embedded = factor * dot(mixed, jnp.concatenate([embedded, embedded], axis=0))
    slope = jnp.mean(d_embedded * pre, axis=-1, keepdims=True)
    d_pre = (inverse * d_embedded - inverse * inverse * inverse * pre * slope).astype(BF16)
    dpre_send[...] = d_pre
    dpre_copy = remote(dpre_send, dpre_recv, 2, partner, mr)
    dpre_copy.start()

    share = (dot(d_pre, weight_buf[...], 1, 1) * scale).astype(BF16)
    pack(dot(adj_t[rows:, :], share), ret_send)
    ret_recv[mg] = ret_send[mg]

    def send_back(i, carry):
        peer = 2 * line_up(lax.div(i, 2)) + lax.rem(i, 2)

        @pl.when(peer != mg)
        def _():
            remote(ret_send.at[peer], ret_recv.at[mg], 3, peer, mr).start()

        return carry

    soon = 3 * near // 2
    lax.fori_loop(0, soon, send_back, 0)

    product = dot(d_pre, mean_mine, 0, 0)
    mean_copy.wait()
    dpre_copy.wait()

    def send_tiles(side):
        part = slice(side * lanes, (side + 1) * lanes)
        both = product[:, part] + dot(dpre_recv[...], mean_recv[:, part], 0, 0)
        tile_send[side] = both.astype(BF16).reshape(replicas, wide, lanes)
        tile_recv[side, mr] = tile_send[side, mr]

        def send_tile(i, carry):
            peer = lax.rem(mr + i, replicas)
            remote(
                tile_send.at[side, peer], tile_recv.at[side, mr], 4 + side, mg, peer
            ).start()
            return carry

        lax.fori_loop(1, replicas, send_tile, 0)

    send_tiles(0)
    send_tiles(1)

    def send_z(i, carry):
        peer = line_up(i)

        @pl.when(peer != chip)
        def _():
            remote(z_send.at[peer], z_recv.at[chip], 6, 2 * peer + core, mr).start()

        return carry

    total[...] = share.astype(F32) + dot(adj_t[:rows, :], share)
    per = LANES // wide

    def plane_sum(side):
        wait_all(tile_recv.at[side], recv_sems.at[4 + side], replicas - 1)
        plane = tile_recv[side, 0].astype(F32)
        for p in range(1, replicas):
            plane = plane + tile_recv[side, p].astype(F32)
        if wide < LANES:
            plane = jnp.concatenate([plane, jnp.zeros((LANES - wide, lanes), F32)], axis=0)
        plane_t = plane.T
        for h in range(tall // per):
            packed = plane_t[h * per * wing : (h * per + 1) * wing, :]
            for i in range(1, per):
                e = h * per + i
                packed = packed + pltpu.roll(
                    plane_t[e * wing : (e + 1) * wing, :], i * wide, axis=1
                )
            for c in range(wing):
                z_send[side * wing + c, h : h + 1, :] = packed[c : c + 1, :]

    plane_sum(0)
    lax.fori_loop(0, wing, send_z, 0)
    lax.fori_loop(soon, 2 * wing, send_back, 0)
    plane_sum(1)
    lax.fori_loop(wing, chips, send_z, 0)
    lax.fori_loop(2 * wing, groups, send_back, 0)
    z_recv[chip] = z_send[chip]

    wait_all(ret_recv, recv_sems.at[3], groups - 1)
    returned = unpack(ret_recv)
    d_rows = total[...]
    for k in range(capacity):
        d_rows = d_rows + dot(sent[k], returned[k * groups : (k + 1) * groups, :])
    d_features[...] = d_rows.astype(BF16)

    wait_all(z_recv, recv_sems.at[6], chips - 1)
    block = jnp.sum(z_recv[...], axis=0) * (1.0 / math.sqrt(groups * replicas))
    for e in range(tall):
        line = block[e // per : e // per + 1, :]
        if e % per:
            line = pltpu.roll(line, LANES - (e % per) * wide, axis=1)
        weight_grad[e : e + 1, :] = line[:, :wide]

    wait_all(out_send, send_sems.at[7], 4 * near - 2)
    wait_all(out_send, send_sems.at[0], groups - 1)
    wait_all(ret_send, send_sems.at[3], groups - 1)
    wait_all(tile_send.at[0], send_sems.at[4], replicas - 1)
    wait_all(tile_send.at[1], send_sems.at[5], replicas - 1)
    wait_all(z_send, send_sems.at[6], chips - 1)


def hand_over(rows, block, rows_out, block_out):
    rows_out[...] = rows[...]
    block_out[...] = block[...]


def body(
    groups, replicas, features, neighbours, send_rows, send_counts, candidates, perturbation, weight
):
    rows, width = features.shape[1:]
    capacity = send_rows.shape[3]
    queries, cands = candidates.shape[1:]
    samples = perturbation.shape[2]
    slots = groups * capacity
    parts = capacity * width // LANES
    tall, wide = width // groups, width // replicas
    chips = groups // 2
    half = tall * chips
    packed = tall * wide // LANES
    args = (
        features[0],
        neighbours[0].T,
        send_rows[0, 0].T,
        send_counts[0],
        candidates[0],
        perturbation[0],
        weight,
    )
    vmem = pl.BlockSpec(memory_space=pltpu.VMEM)
    message = pltpu.VMEM((groups, parts, LANES), BF16)
    d_features, weight_grad = pl.pallas_call(
        functools.partial(kernel, groups, replicas),
        name="layer",
        out_shape=(
            jax.ShapeDtypeStruct((rows, width), BF16),
            jax.ShapeDtypeStruct((tall, wide), F32),
        ),
        in_specs=[pl.BlockSpec(memory_space=pl.ANY)] * 7,
        out_specs=(vmem, vmem),
        scratch_shapes=[pltpu.VMEM(x.shape, x.dtype) for x in args]
        + [
            pltpu.VMEM((groups * parts, LANES), F32),
            pltpu.VMEM((2 * groups, parts, LANES), BF16),
            message,
            pltpu.VMEM((2, chips // 2, parts, LANES), BF16),
            message,
            message,
            pltpu.VMEM((rows, half), BF16),
            pltpu.VMEM((rows, half), BF16),
            pltpu.VMEM((rows, width), BF16),
            pltpu.VMEM((rows, width), BF16),
            pltpu.VMEM((2, replicas, wide, half // 2), BF16),
            pltpu.VMEM((2, replicas, wide, half // 2), BF16),
            pltpu.VMEM((chips, packed, LANES), F32),
            pltpu.VMEM((chips, packed, LANES), F32),
            pltpu.VMEM((rows, rows + slots), BF16),
            pltpu.VMEM((rows + slots, rows), BF16),
            pltpu.VMEM((queries * rows, cands), BF16),
            pltpu.VMEM((samples, queries, cands), F32),
            pltpu.VMEM((rows, width), F32),
            pltpu.SemaphoreType.DMA((8,)),
            pltpu.SemaphoreType.DMA((8,)),
            pltpu.SemaphoreType.DMA((7,)),
            pltpu.SemaphoreType.DMA((2, chips // 4)),
        ],
        compiler_params=pltpu.CompilerParams(
            collective_id=0, has_side_effects=True, vmem_limit_bytes=56 * 1024 * 1024
        ),
    )(*args)
    d_features, weight_grad = pl.pallas_call(
        hand_over,
        name="hand_over",
        out_shape=(
            jax.ShapeDtypeStruct((rows, width), BF16),
            jax.ShapeDtypeStruct((tall, wide), F32),
        ),
        in_specs=[vmem] * 2,
        out_specs=(vmem, vmem),
    )(d_features, weight_grad)
    return d_features[None], weight_grad


def solution(mesh):
    placed = (
        P("replica", "graph", None),
        P("replica", "graph", None),
        P("replica", "graph", None, None),
        P("replica", "graph", None),
        P("replica", "graph", None),
        P("replica", "graph", None, None),
        P(),
    )
    return jax.shard_map(
        functools.partial(body, mesh.shape["graph"], mesh.shape["replica"]),
        mesh=mesh,
        in_specs=placed,
        out_specs=(P("replica", "graph", None), P("graph", "replica")),
        check_vma=False,
    )
```

time: 77.5 us -> 70.1 us (0.905)
  the two profiles are of different devices: /device:TPU:1 before, /device:TPU:56 now
where the time goes in v2:
time: 70.1 us; the launch traced here: 70 us
  Pallas kernels  69.3 us (99%)
    pallas_call x1, Pallas kernels, body(): pl.pallas_call(functools.partial(kernel, groups, replicas), name='layer',...  67.8 us
    pallas_call x1, Pallas kernels, body(): pl.pallas_call(hand_over, name='hand_over', out_shape=(jax.ShapeDtypeStru...  1.57 us

profile of v2, /device:TPU:56, one launch (start us, length us, event | category | flops | bytes accessed | tf_op | source)
XLA Modules:
  0.0 70.0 jit_solution(16664669320293363425)
XLA Ops:
  0.6 67.8 %layer.1 = (bf16[128,512]{1,0:T(8,128)(2,1)}, f32[8,32]{1,0:T(8,128)}) custom-call(bf16[128,512]{1,0:T(8,128)(2,1)} %bitcast.12, s32[16,128]{1,0:T(8,128)} %bitcast.14, s32[2,64]{1,0:T(2,128)} %bitcast.15, s32[1,64]{1,0:T(1,128)} %bitcast.16, s32[32,512]{1,0:T(8,128)} %bitcast.13, f32[32,4,512]{2,1,0:T(4,128)} %bitcast.11, bf16[512,512]{1,0:T(8,128)(2,1)} %weight.1), custom_call_target="tpu_custom_call" | custom-call | tf_op jit(solution)/shard_map/layer/pallas_call | solution.py:480
  68.4 1.6 %hand_over.1 = (bf16[128,512]{1,0:T(8,128)(2,1)}, f32[8,32]{1,0:T(8,128)}) custom-call(bf16[128,512]{1,0:T(8,128)(2,1)} %get-tuple-element.6.rows, f32[8,32]{1,0:T(8,128)} %get-tuple-element.7.block), custom_call_target="tpu_custom_call" | custom-call | tf_op jit(solution)/shard_map/hand_over/pallas_call | solution.py:519

commit v3 on v2

--- a/solution.py
+++ b/solution.py
@@ -349,10 +349,6 @@
     dpre_copy = remote(dpre_send, dpre_recv, 2, partner, mr)
     dpre_copy.start()
 
-    share = (dot(d_pre, weight_buf[...], 1, 1) * scale).astype(BF16)
-    pack(dot(adj_t[rows:, :], share), ret_send)
-    ret_recv[mg] = ret_send[mg]
-
     def send_back(i, carry):
         peer = 2 * line_up(lax.div(i, 2)) + lax.rem(i, 2)
 
@@ -362,12 +358,19 @@
 
         return carry
 
-    soon = 3 * near // 2
-    lax.fori_loop(0, soon, send_back, 0)
 
     product = dot(d_pre, mean_mine, 0, 0)
     mean_copy.wait()
     dpre_copy.wait()
+
+    across = math.isqrt(replicas)
+    steps = sorted(
+        ((dx, dy) for dx in range(across) for dy in range(across) if dx or dy),
+        key=lambda step: (
+            -sum(min(d, across - d) for d in step),
+            min(step[0], across - step[0]) - min(step[1], across - step[1]),
+        ),
+    )
 
     def send_tiles(side):
         part = slice(side * lanes, (side + 1) * lanes)
@@ -375,17 +378,19 @@
         tile_send[side] = both.astype(BF16).reshape(replicas, wide, lanes)
         tile_recv[side, mr] = tile_send[side, mr]
 
-        def send_tile(i, carry):
-            peer = lax.rem(mr + i, replicas)
+        for dx, dy in steps:
+            peer = lax.rem(mr // across + dx, across) * across + lax.rem(mr + dy, across)
             remote(
                 tile_send.at[side, peer], tile_recv.at[side, mr], 4 + side, mg, peer
             ).start()
-            return carry
-
-        lax.fori_loop(1, replicas, send_tile, 0)
 
     send_tiles(0)
     send_tiles(1)
+
+    share = (dot(d_pre, weight_buf[...], 1, 1) * scale).astype(BF16)
+    pack(dot(adj_t[rows:, :], share), ret_send)
+    ret_recv[mg] = ret_send[mg]
+
 
     def send_z(i, carry):
         peer = line_up(i)
@@ -417,6 +422,8 @@
             for c in range(wing):
                 z_send[side * wing + c, h : h + 1, :] = packed[c : c + 1, :]
 
+    soon = 16
+    lax.fori_loop(0, soon, send_back, 0)
     plane_sum(0)
     lax.fori_loop(0, wing, send_z, 0)
     lax.fori_loop(soon, 2 * wing, send_back, 0)

time: 70.1 us -> 69.1 us (0.986)
  the two profiles are of different devices: /device:TPU:56 before, /device:TPU:2 now
where the time goes in v3:
time: 69.1 us; the launch traced here: 69 us
  Pallas kernels  68.3 us (99%)
    pallas_call x1, Pallas kernels, body(): pl.pallas_call(functools.partial(kernel, groups, replicas), name='layer',...  66.7 us
    pallas_call x1, Pallas kernels, body(): pl.pallas_call(hand_over, name='hand_over', out_shape=(jax.ShapeDtypeStru...  1.57 us

profile of v3, /device:TPU:2, one launch (start us, length us, event | category | flops | bytes accessed | tf_op | source)
XLA Modules:
  0.0 69.0 jit_solution(15367783120193550185)
XLA Ops:
  0.6 66.7 %layer.1 = (bf16[128,512]{1,0:T(8,128)(2,1)}, f32[8,32]{1,0:T(8,128)}) custom-call(bf16[128,512]{1,0:T(8,128)(2,1)} %bitcast.12, s32[16,128]{1,0:T(8,128)} %bitcast.14, s32[2,64]{1,0:T(2,128)} %bitcast.15, s32[1,64]{1,0:T(1,128)} %bitcast.16, s32[32,512]{1,0:T(8,128)} %bitcast.13, f32[32,4,512]{2,1,0:T(4,128)} %bitcast.11, bf16[512,512]{1,0:T(8,128)(2,1)} %weight.1), custom_call_target="tpu_custom_call" | custom-call | tf_op jit(solution)/shard_map/layer/pallas_call | solution.py:487
  67.4 1.6 %hand_over.1 = (bf16[128,512]{1,0:T(8,128)(2,1)}, f32[8,32]{1,0:T(8,128)}) custom-call(bf16[128,512]{1,0:T(8,128)(2,1)} %get-tuple-element.6.rows, f32[8,32]{1,0:T(8,128)} %get-tuple-element.7.block), custom_call_target="tpu_custom_call" | custom-call | tf_op jit(solution)/shard_map/hand_over/pallas_call | solution.py:526

commit v4 on v3

--- a/solution.py
+++ b/solution.py
@@ -79,6 +79,7 @@
     recv_sems,
     load_sems,
     relay_sems,
+    row_out,
 ):
     mg = lax.axis_index("graph")
     mr = lax.axis_index("replica")
@@ -359,6 +360,21 @@
         return carry
 
 
+    share = (dot(d_pre, weight_buf[...], 1, 1) * scale).astype(BF16)
+    pack(dot(adj_t[rows:, :], share), ret_send)
+    ret_recv[mg] = ret_send[mg]
+
+
+    def send_z(i, carry):
+        peer = line_up(i)
+
+        @pl.when(peer != chip)
+        def _():
+            remote(z_send.at[peer], z_recv.at[chip], 6, 2 * peer + core, mr).start()
+
+        return carry
+
+
     product = dot(d_pre, mean_mine, 0, 0)
     mean_copy.wait()
     dpre_copy.wait()
@@ -387,21 +403,6 @@
     send_tiles(0)
     send_tiles(1)
 
-    share = (dot(d_pre, weight_buf[...], 1, 1) * scale).astype(BF16)
-    pack(dot(adj_t[rows:, :], share), ret_send)
-    ret_recv[mg] = ret_send[mg]
-
-
-    def send_z(i, carry):
-        peer = line_up(i)
-
-        @pl.when(peer != chip)
-        def _():
-            remote(z_send.at[peer], z_recv.at[chip], 6, 2 * peer + core, mr).start()
-
-        return carry
-
-    total[...] = share.astype(F32) + dot(adj_t[:rows, :], share)
     per = LANES // wide
 
     def plane_sum(side):
@@ -422,8 +423,9 @@
             for c in range(wing):
                 z_send[side * wing + c, h : h + 1, :] = packed[c : c + 1, :]
 
-    soon = 16
+    soon = 3 * groups // 16
     lax.fori_loop(0, soon, send_back, 0)
+    total[...] = share.astype(F32) + dot(adj_t[:rows, :], share)
     plane_sum(0)
     lax.fori_loop(0, wing, send_z, 0)
     lax.fori_loop(soon, 2 * wing, send_back, 0)
@@ -437,7 +439,9 @@
     d_rows = total[...]
     for k in range(capacity):
         d_rows = d_rows + dot(sent[k], returned[k * groups : (k + 1) * groups, :])
-    d_features[...] = d_rows.astype(BF16)
+    row_out[...] = d_rows.astype(BF16)
+    out_copy = pltpu.make_async_copy(row_out, d_features, load_sems.at[0])
+    out_copy.start()
 
     wait_all(z_recv, recv_sems.at[6], chips - 1)
     block = jnp.sum(z_recv[...], axis=0) * (1.0 / math.sqrt(groups * replicas))
@@ -450,6 +454,7 @@
     wait_all(out_send, send_sems.at[7], 4 * near - 2)
     wait_all(out_send, send_sems.at[0], groups - 1)
     wait_all(ret_send, send_sems.at[3], groups - 1)
+    out_copy.wait()
     wait_all(tile_send.at[0], send_sems.at[4], replicas - 1)
     wait_all(tile_send.at[1], send_sems.at[5], replicas - 1)
     wait_all(z_send, send_sems.at[6], chips - 1)
@@ -492,7 +497,7 @@
             jax.ShapeDtypeStruct((tall, wide), F32),
         ),
         in_specs=[pl.BlockSpec(memory_space=pl.ANY)] * 7,
-        out_specs=(vmem, vmem),
+        out_specs=(pl.BlockSpec(memory_space=pl.ANY), vmem),
         scratch_shapes=[pltpu.VMEM(x.shape, x.dtype) for x in args]
         + [
             pltpu.VMEM((groups * parts, LANES), F32),
@@ -518,6 +523,7 @@
             pltpu.SemaphoreType.DMA((8,)),
             pltpu.SemaphoreType.DMA((7,)),
             pltpu.SemaphoreType.DMA((2, chips // 4)),
+            pltpu.VMEM((rows, width), BF16),
         ],
         compiler_params=pltpu.CompilerParams(
             collective_id=0, has_side_effects=True, vmem_limit_bytes=56 * 1024 * 1024

time: 69.1 us -> 69 us (level)
  the two profiles are of different devices: /device:TPU:2 before, /device:TPU:56 now
where the time goes in v4:
time: 69 us; the launch traced here: 68.8 us
  Pallas kernels  68.2 us (99%)
    pallas_call x1, Pallas kernels, body(): pl.pallas_call(functools.partial(kernel, groups, replicas), name='layer',...  66.6 us
    pallas_call x1, Pallas kernels, body(): pl.pallas_call(hand_over, name='hand_over', out_shape=(jax.ShapeDtypeStru...  1.57 us

profile of v4, /device:TPU:56, one launch (start us, length us, event | category | flops | bytes accessed | tf_op | source)
XLA Modules:
  0.0 68.8 jit_solution(5863271413093805392)
XLA Ops:
  0.6 66.6 %layer.1 = (bf16[128,512]{1,0:T(8,128)(2,1)}, f32[8,32]{1,0:T(8,128)}) custom-call(bf16[128,512]{1,0:T(8,128)(2,1)} %bitcast.12, s32[16,128]{1,0:T(8,128)} %bitcast.14, s32[2,64]{1,0:T(2,128)} %bitcast.15, s32[1,64]{1,0:T(1,128)} %bitcast.16, s32[32,512]{1,0:T(8,128)} %bitcast.13, f32[32,4,512]{2,1,0:T(4,128)} %bitcast.11, bf16[512,512]{1,0:T(8,128)(2,1)} %weight.1), custom_call_target="tpu_custom_call" | custom-call | tf_op jit(solution)/shard_map/layer/pallas_call | solution.py:492
  67.3 1.6 %hand_over.1 = (bf16[128,512]{1,0:T(8,128)(2,1)}, f32[8,32]{1,0:T(8,128)}) custom-call(bf16[128,512]{1,0:T(8,128)(2,1)} %get-tuple-element.6.rows, f32[8,32]{1,0:T(8,128)} %get-tuple-element.7.block), custom_call_target="tpu_custom_call" | custom-call | tf_op jit(solution)/shard_map/hand_over/pallas_call | solution.py:532
